TPU v7x, 32 devices: a whole 2x2x4 slice. The times are simulated.
32 devices in a mesh: grp: 2 (over y), aux: 16 (over z, x, core).
Axes of the slice: x: 2, y: 2, z: 4, core: 2. Of those that a mesh axis runs over, the one named last changes fastest.
Arguments:
- rhs: float32 [512, 2, 1024], P(('grp', 'aux')), parts along dimension 0, may hold values from -6 to 6
- occ_energy: float32 [512], P('grp'), parts along dimension 0, may hold values from -1.5 to -0.3
- vir_energy: float32 [2048], P('grp'), parts along dimension 0, may hold values from 0.2 to 3
- occ_ints: bfloat16 [128, 256, 256], P(('grp', 'aux')), parts along dimension 0, may hold values from -0.046875 to 0.046875
- vir_ints: bfloat16 [128, 1024, 1024], P(('grp', 'aux')), parts along dimension 0, may hold values from -0.1875 to 0.1875
Outputs:
- response: float32 [512, 2, 1024], P(('grp', 'aux')), parts along dimension 0
There are 2 independent parts, one for each index of `grp`. A program takes and returns all parts, laid end to end along the dimension named above; each array names one. Nothing has to cross between parts.
All inputs are finite; a program needn't handle non-finite values.
Results may differ from a plain program's by a relative error of at most 0.0015.
Values may be sent and summed in bfloat16 or wider, within the bound.
A program may use at most 64 MiB of HBM per device.

v0:
```python
import functools

import jax
import jax.numpy as jnp
from jax import lax
from jax.experimental import pallas as pl
from jax.experimental.pallas import tpu as pltpu
from jax.sharding import PartitionSpec as P

ITERS = 2
CHUNKS = 2
MESH = pl.DeviceIdType.MESH
F32 = jnp.float32
BF16 = jnp.bfloat16


def kernel(
    nz, rhs_hbm, occ_e_hbm, vir_e_hbm, occ_hbm, vir_hbm, out,
    rhs, occ_e, vir_e, occ_v, vir_v, vir_t, denom, resp, ag, half, ex, cr, xo, xs, xr, zo, zs, zr,
    load_sem, agz_s, agz_r, agx_s, agx_r, agc_s, agc_r,
    rc_s, rc_r, rx_s, rx_r, rz_s, rz_r,
):
    rows, states, nvir = rhs.shape
    nocc = half.shape[0]
    local_aux = occ_v.shape[0]
    width = nvir // CHUNKS
    grp = lax.axis_index("grp")
    me = lax.axis_index("aux")
    c = lax.rem(me, 2)
    x = lax.rem(me // 2, 2)
    z = me // 4

    def dev(zz, xx, cc):
        return (grp, (zz * 2 + xx) * 2 + cc)

    def up(k):
        return lax.rem(z + k, nz)

    def down(k):
        return lax.rem(z + nz - k, nz)

    sibling = dev(z, x, 1 - c)
    across = dev(z, 1 - x, c)

    pairs = [(rhs_hbm, rhs), (occ_e_hbm, occ_e), (vir_e_hbm, vir_e), (occ_hbm, occ_v)]
    pairs += [(vir_hbm.at[p], vir_v.at[p]) for p in range(local_aux)]
    loads = [pltpu.make_async_copy(src, dst, load_sem.at[i]) for i, (src, dst) in enumerate(pairs)]
    for load in loads:
        load.start()

    barrier = pltpu.get_barrier_semaphore()
    for peer in [sibling, across] + [dev(up(k), x, c) for k in range(1, nz)]:
        pl.semaphore_signal(barrier, inc=1, device_id=peer, device_id_type=MESH)

    for load in loads[:3]:
        load.wait()
    picked = lax.broadcasted_iota(jnp.int32, (rows, nocc), 1) == (
        lax.broadcasted_iota(jnp.int32, (rows, nocc), 0) + me * rows
    )
    own_occ = jnp.sum(jnp.where(picked, occ_e[...], 0.0), axis=1, keepdims=True)
    denom[...] = vir_e[...] - own_occ
    for s in range(states):
        resp[s] = rhs[:, s, :] / denom[...]
    pl.semaphore_wait(barrier, nz + 1)

    sent = []

    def send(src, dst, s_sem, r_sem, to):
        copy = pltpu.make_async_remote_copy(
            src_ref=src, dst_ref=dst, send_sem=s_sem, recv_sem=r_sem, device_id=to, device_id_type=MESH
        )
        copy.start()
        sent.append(copy)

    def arrived(dst, s_sem, r_sem, frm):
        pltpu.make_async_remote_copy(
            src_ref=dst, dst_ref=dst, send_sem=s_sem, recv_sem=r_sem, device_id=frm, device_id_type=MESH
        ).wait_recv()

    near_first = sorted(range(1, nz), key=lambda k: min(k, nz - k))

    def ag_start(it, s):
        block = ag.at[it, s, z, x, c]
        block[...] = resp[s].astype(BF16)
        for k in near_first:
            send(block, block, agz_s.at[it, s, k], agz_r.at[it, s, k], dev(up(k), x, c))
        send(block, block, agx_s.at[it, s, 0], agx_r.at[it, s, 0], across)

    def ag_z(it, s):
        for k in near_first:
            block = ag.at[it, s, down(k), x, c]
            arrived(block, agz_s.at[it, s, k], agz_r.at[it, s, k], dev(down(k), x, c))
            send(block, block, agx_s.at[it, s, k], agx_r.at[it, s, k], across)
        line = ag.at[it, s, :, x, c]
        send(line, line, agc_s.at[it, s, 0], agc_r.at[it, s, 0], sibling)

    def ag_x(it, s):
        for k in [0] + near_first:
            block = ag.at[it, s, down(k), 1 - x, c]
            arrived(block, agx_s.at[it, s, k], agx_r.at[it, s, k], across)
        line = ag.at[it, s, :, 1 - x, c]
        send(line, line, agc_s.at[it, s, 1], agc_r.at[it, s, 1], sibling)

    def ag_c(it, s):
        arrived(ag.at[it, s, :, x, 1 - c], agc_s.at[it, s, 0], agc_r.at[it, s, 0], sibling)
        arrived(ag.at[it, s, :, 1 - x, 1 - c], agc_s.at[it, s, 1], agc_r.at[it, s, 1], sibling)

    def halves(it, s):
        gathered = ag[it, s].reshape(nocc, nvir)
        product = jnp.dot(occ_v[...].reshape(local_aux * nocc, nocc), gathered, preferred_element_type=F32)
        for p in range(local_aux):
            half[:, pl.ds(p * nvir, nvir)] = product[p * nocc : (p + 1) * nocc].astype(BF16)

    def turn(p):
        loads[4 + p].wait()
        vir_t[pl.ds(p * nvir, nvir), :] = vir_v[p].T

    def exchange(it, s, ch):
        cols = pl.ds(ch * width, width)
        product = jnp.dot(half[...], vir_t[:, cols], preferred_element_type=F32)
        ex[it, s, :, :, :, :, cols] = product.reshape(nz, 2, 2, rows, width)
        send(
            ex.at[it, s, :, :, 1 - c, :, cols], cr.at[it, s, :, :, :, cols],
            rc_s.at[it, s, ch], rc_r.at[it, s, ch], sibling,
        )

    def rs_x(it, s, ch):
        cols = pl.ds(ch * width, width)
        arrived(cr.at[it, s, :, :, :, cols], rc_s.at[it, s, ch], rc_r.at[it, s, ch], sibling)
        xs[it, s, :, :, cols] = (
            ex[it, s, :, 1 - x, c, :, cols] + cr[it, s, :, 1 - x, :, cols]
        ).astype(BF16)
        send(
            xs.at[it, s, :, :, cols], xr.at[it, s, :, :, cols],
            rx_s.at[it, s, ch], rx_r.at[it, s, ch], across,
        )
        xo[s, :, :, cols] = ex[it, s, :, x, c, :, cols] + cr[it, s, :, x, :, cols]

    def rs_z(it, s, ch):
        cols = pl.ds(ch * width, width)
        arrived(xr.at[it, s, :, :, cols], rx_s.at[it, s, ch], rx_r.at[it, s, ch], across)
        for k in near_first[::-1]:
            zs[it, s, k, :, cols] = (xo[s, up(k), :, cols] + xr[it, s, up(k), :, cols].astype(F32)).astype(BF16)
            send(
                zs.at[it, s, k, :, cols], zr.at[it, s, k, :, cols],
                rz_s.at[it, s, ch, k], rz_r.at[it, s, ch, k], dev(up(k), x, c),
            )
        zo[s, :, cols] = xo[s, z, :, cols] + xr[it, s, z, :, cols].astype(F32)

    def rs_end(it, s):
        for ch in range(CHUNKS):
            cols = pl.ds(ch * width, width)
            total = zo[s, :, cols]
            for k in near_first:
                arrived(zr.at[it, s, k, :, cols], rz_s.at[it, s, ch, k], rz_r.at[it, s, ch, k], dev(down(k), x, c))
                total = total + zr[it, s, k, :, cols].astype(F32)
            new = 0.4 * resp[s, :, cols] + 0.6 * (rhs[:, s, cols] - total) / denom[:, cols]
            if it == ITERS - 1:
                out[:, s, cols] = new
            else:
                resp[s, :, cols] = new

    a, b = 0, 1
    ag_start(0, a)
    ag_start(0, b)
    first, second = local_aux // 2, local_aux
    for p in range(first):
        turn(p)
    ag_z(0, a)
    for p in range(first, second):
        turn(p)
    ag_x(0, a)
    ag_z(0, b)
    ag_c(0, a)
    loads[3].wait()
    for it in range(ITERS):
        halves(it, a)
        if it > 0:
            ag_z(it, b)
        exchange(it, a, 0)
        ag_x(it, b)
        exchange(it, a, 1)
        rs_x(it, a, 0)
        ag_c(it, b)
        halves(it, b)
        rs_x(it, a, 1)
        rs_z(it, a, 0)
        exchange(it, b, 0)
        rs_z(it, a, 1)
        rs_x(it, b, 0)
        exchange(it, b, 1)
        rs_end(it, a)
        if it + 1 < ITERS:
            ag_start(it + 1, a)
        rs_x(it, b, 1)
        rs_z(it, b, 0)
        rs_z(it, b, 1)
        if it + 1 < ITERS:
            ag_z(it + 1, a)
        rs_end(it, b)
        if it + 1 < ITERS:
            ag_start(it + 1, b)
            ag_x(it + 1, a)
            ag_c(it + 1, a)
    for copy in sent:
        copy.wait_send()


def fused(rhs, occ_energy, vir_energy, occ_ints, vir_ints, devices):
    rows, states, nvir = rhs.shape
    local_aux, nocc, _ = occ_ints.shape
    nz = devices // 4
    dma = pltpu.SemaphoreType.DMA
    vmem = pl.BlockSpec(memory_space=pltpu.VMEM)
    hbm = pl.BlockSpec(memory_space=pltpu.HBM)
    lead = (ITERS, states)
    pair = lambda *shape: [dma(lead + shape)] * 2
    flops = ITERS * 2 * local_aux * nocc * states * nvir * (nocc + nvir)
    return pl.pallas_call(
        functools.partial(kernel, nz),
        out_shape=jax.ShapeDtypeStruct(rhs.shape, F32),
        in_specs=[hbm] * 5,
        out_specs=vmem,
        scratch_shapes=[
            pltpu.VMEM(rhs.shape, F32),
            pltpu.VMEM((1, nocc), F32),
            pltpu.VMEM((1, nvir), F32),
            pltpu.VMEM(occ_ints.shape, BF16),
            pltpu.VMEM(vir_ints.shape, BF16),
            pltpu.VMEM((local_aux * nvir, nvir), BF16),
            pltpu.VMEM((rows, nvir), F32),
            pltpu.VMEM((states, rows, nvir), F32),
            pltpu.VMEM(lead + (nz, 2, 2, rows, nvir), BF16),
            pltpu.VMEM((nocc, local_aux * nvir), BF16),
            pltpu.VMEM(lead + (nz, 2, 2, rows, nvir), F32),
            pltpu.VMEM(lead + (nz, 2, rows, nvir), F32),
            pltpu.VMEM((states, nz, rows, nvir), F32),
            pltpu.VMEM(lead + (nz, rows, nvir), BF16),
            pltpu.VMEM(lead + (nz, rows, nvir), BF16),
            pltpu.VMEM((states, rows, nvir), F32),
            pltpu.VMEM(lead + (nz, rows, nvir), BF16),
            pltpu.VMEM(lead + (nz, rows, nvir), BF16),
            dma((local_aux + 4,)),
            *pair(nz), *pair(nz), *pair(2),
            *pair(CHUNKS), *pair(CHUNKS), *pair(CHUNKS, nz),
        ],
        compiler_params=pltpu.CompilerParams(
            collective_id=0, has_side_effects=True, vmem_limit_bytes=52 * 2**20
        ),
        cost_estimate=pl.CostEstimate(flops=flops, bytes_accessed=2 * vir_ints.size, transcendentals=0),
    )(rhs, occ_energy.reshape(1, nocc), vir_energy.reshape(1, nvir), occ_ints, vir_ints)


def collective(rhs, occ_energy, vir_energy, occ_ints, vir_ints):
    own_rows, states, nvir = rhs.shape
    local_aux, nocc, _ = occ_ints.shape
    position = lax.axis_index("aux")
    my_occ = lax.dynamic_slice_in_dim(occ_energy, position * own_rows, own_rows, 0)
    denom = vir_energy[None, None, :] - my_occ[:, None, None]
    response = rhs / denom
    for step in range(ITERS):
        rounded = response.astype(BF16)
        piece = lax.all_gather(rounded, "aux", axis=0, tiled=True)
        flat = piece.reshape(piece.shape[0], states * nvir)
        half = jnp.einsum("pij,jk->pik", occ_ints, flat, preferred_element_type=F32)
        half = half.astype(BF16).reshape(local_aux, nocc, states, nvir)
        exchange = lax.psum_scatter(
            lax.dot_general(half, vir_ints, (((0, 3), (0, 2)), ((), ())), preferred_element_type=F32),
            "aux", scatter_dimension=0, tiled=True,
        )
        response = 0.4 * response + 0.6 * (rhs - exchange) / denom
    return response


def solution(mesh):
    devices = mesh.shape["aux"]

    def shards(rhs, occ_energy, vir_energy, occ_ints, vir_ints):
        rows, states, nvir = rhs.shape
        if rows % 16 == 0 and devices % 4 == 0 and devices > 4 and states == 2:
            return fused(rhs, occ_energy, vir_energy, occ_ints, vir_ints, devices)
        return collective(rhs, occ_energy, vir_energy, occ_ints, vir_ints)

    split = P(("grp", "aux"), None, None)
    return jax.shard_map(
        shards, mesh=mesh, in_specs=(split, P("grp"), P("grp"), split, split), out_specs=split, check_vma=False
    )
```

profile of v0, /device:TPU:0, one launch (start us, length us, event | category | flops | bytes accessed | tf_op | source)
XLA Modules:
  0.0 67.1 jit_solution(8729858473035224071)
XLA Ops:
  0.0 0.0 copy-start
  0.0 1.0 %copy-done = bf16[4,256,256]{2,1,0:T(8,128)(2,1)S(1)} copy-done((bf16[4,256,256]{2,1,0:T(8,128)(2,1)S(1)}, bf16[4,256,256]{2,1,0:T(8,128)(2,1)}, u32[]{:S(2)}) %copy-start) | copy-done | bytes 524312
  1.0 0.0 copy-start.1
  1.0 0.9 %copy-done.1 = f32[16,2,1024]{2,1,0:T(2,128)S(1)} copy-done((f32[16,2,1024]{2,1,0:T(2,128)S(1)}, f32[16,2,1024]{2,1,0:T(2,128)}, u32[]{:S(2)}) %copy-start.1) | copy-done | bytes 131096
  1.9 0.0 copy-start.2
  1.9 0.7 %copy-done.2 = f32[1024]{0:T(1024)S(1)} copy-done((f32[1024]{0:T(1024)S(1)}, f32[1024]{0:T(1024)}, u32[]{:S(2)}) %copy-start.2) | copy-done | bytes 4120
  2.6 0.0 copy-start.3
  2.6 0.7 %copy-done.3 = f32[256]{0:T(256)S(1)} copy-done((f32[256]{0:T(256)S(1)}, f32[256]{0:T(256)}, u32[]{:S(2)}) %copy-start.3) | copy-done | bytes 1048
  3.3 63.1 %shard_map.55 = f32[16,2,1024]{2,1,0:T(2,128)S(1)} custom-call(f32[16,2,1024]{2,1,0:T(2,128)S(1)} %copy-done.1, f32[1,256]{1,0:T(1,128)S(1)} %bitcast.3, f32[1,1024]{1,0:T(1,128)S(1)} %bitcast.2, bf16[4,256,256]{2,1,0:T(8,128)(2,1)S(1)} %copy-done, bf16[4,1024,1024]{2,1,0:T(8,128)(2,1)} %vir_hbm.1), custom_call_target="tpu_custom_call" | custom-call | flops 10737418240 | bytes 8388608 | tf_op jit(solution)/shard_map/pallas_call | solution.py:219
  66.4 0.7 copy.7
Async XLA Ops:
  0.0 1.0 %copy-start = (bf16[4,256,256]{2,1,0:T(8,128)(2,1)S(1)}, bf16[4,256,256]{2,1,0:T(8,128)(2,1)}, u32[]{:S(2)}) copy-start(bf16[4,256,256]{2,1,0:T(8,128)(2,1)} %occ_hbm.1) | copy-start | bytes 1572868
  1.0 0.9 %copy-start.1 = (f32[16,2,1024]{2,1,0:T(2,128)S(1)}, f32[16,2,1024]{2,1,0:T(2,128)}, u32[]{:S(2)}) copy-start(f32[16,2,1024]{2,1,0:T(2,128)} %rhs_hbm.1) | copy-start | bytes 393220
  1.9 0.7 %copy-start.2 = (f32[1024]{0:T(1024)S(1)}, f32[1024]{0:T(1024)}, u32[]{:S(2)}) copy-start(f32[1024]{0:T(1024)} %param.7) | copy-start | bytes 12292
  2.6 0.7 %copy-start.3 = (f32[256]{0:T(256)S(1)}, f32[256]{0:T(256)}, u32[]{:S(2)}) copy-start(f32[256]{0:T(256)} %param.6) | copy-start | bytes 3076
where the time goes:
time: 67.3 us; the launch traced here: 67.1 us
  Pallas kernels  63.1 us (94%)
  local copies, waits for them, and re-layouts  3.97 us (6%)
    pallas_call x1, Pallas kernels, fused(): pl.pallas_call(functools.partial(kernel, nz), out_shape=jax.ShapeDtypeStr...  63.1 us
    unnamed x9, local copies, waits for them, and re-layouts  3.97 us

commit v1 on v0

--- a/solution.py
+++ b/solution.py
@@ -16,12 +16,12 @@
 
 def kernel(
     nz, rhs_hbm, occ_e_hbm, vir_e_hbm, occ_hbm, vir_hbm, out,
-    rhs, occ_e, vir_e, occ_v, vir_v, vir_t, denom, resp, ag, half, ex, cr, xo, xs, xr, zo, zs, zr,
+    rhs, occ_e, vir_e, occ_v, vir_v, denom, resp, ag, half, ex, cr, xo, xs, xr, zo, zs, zr,
     load_sem, agz_s, agz_r, agx_s, agx_r, agc_s, agc_r,
     rc_s, rc_r, rx_s, rx_r, rz_s, rz_r,
 ):
     rows, states, nvir = rhs.shape
-    nocc = half.shape[0]
+    nocc = half.shape[1]
     local_aux = occ_v.shape[0]
     width = nvir // CHUNKS
     grp = lax.axis_index("grp")
@@ -43,7 +43,7 @@
     across = dev(z, 1 - x, c)
 
     pairs = [(rhs_hbm, rhs), (occ_e_hbm, occ_e), (vir_e_hbm, vir_e), (occ_hbm, occ_v)]
-    pairs += [(vir_hbm.at[p], vir_v.at[p]) for p in range(local_aux)]
+    pairs += [(vir_hbm.at[p], vir_v.at[:, pl.ds(p * nvir, nvir)]) for p in range(local_aux)]
     loads = [pltpu.make_async_copy(src, dst, load_sem.at[i]) for i, (src, dst) in enumerate(pairs)]
     for load in loads:
         load.start()
@@ -79,45 +79,52 @@
 
     near_first = sorted(range(1, nz), key=lambda k: min(k, nz - k))
 
-    def ag_start(it, s):
-        block = ag.at[it, s, z, x, c]
-        block[...] = resp[s].astype(BF16)
+    def ag_start(it, s, ch):
+        cols = pl.ds(ch * width, width)
+        block = ag.at[it, s, z, x, c, :, cols]
+        block[...] = resp[s, :, cols].astype(BF16)
+        for k in near_first[::-1]:
+            send(block, block, agz_s.at[it, s, ch, k], agz_r.at[it, s, ch, k], dev(up(k), x, c))
+        send(block, block, agx_s.at[it, s, ch, 0], agx_r.at[it, s, ch, 0], across)
+
+    def ag_z(it, s, ch):
+        cols = pl.ds(ch * width, width)
         for k in near_first:
-            send(block, block, agz_s.at[it, s, k], agz_r.at[it, s, k], dev(up(k), x, c))
-        send(block, block, agx_s.at[it, s, 0], agx_r.at[it, s, 0], across)
-
-    def ag_z(it, s):
-        for k in near_first:
-            block = ag.at[it, s, down(k), x, c]
-            arrived(block, agz_s.at[it, s, k], agz_r.at[it, s, k], dev(down(k), x, c))
-            send(block, block, agx_s.at[it, s, k], agx_r.at[it, s, k], across)
-        line = ag.at[it, s, :, x, c]
-        send(line, line, agc_s.at[it, s, 0], agc_r.at[it, s, 0], sibling)
-
-    def ag_x(it, s):
+            block = ag.at[it, s, down(k), x, c, :, cols]
+            arrived(block, agz_s.at[it, s, ch, k], agz_r.at[it, s, ch, k], dev(down(k), x, c))
+            send(block, block, agx_s.at[it, s, ch, k], agx_r.at[it, s, ch, k], across)
+        line = ag.at[it, s, :, x, c, :, cols]
+        send(line, line, agc_s.at[it, s, ch, 0], agc_r.at[it, s, ch, 0], sibling)
+
+    def ag_x(it, s, ch):
+        cols = pl.ds(ch * width, width)
         for k in [0] + near_first:
-            block = ag.at[it, s, down(k), 1 - x, c]
-            arrived(block, agx_s.at[it, s, k], agx_r.at[it, s, k], across)
-        line = ag.at[it, s, :, 1 - x, c]
-        send(line, line, agc_s.at[it, s, 1], agc_r.at[it, s, 1], sibling)
-
-    def ag_c(it, s):
-        arrived(ag.at[it, s, :, x, 1 - c], agc_s.at[it, s, 0], agc_r.at[it, s, 0], sibling)
-        arrived(ag.at[it, s, :, 1 - x, 1 - c], agc_s.at[it, s, 1], agc_r.at[it, s, 1], sibling)
-
-    def halves(it, s):
-        gathered = ag[it, s].reshape(nocc, nvir)
+            block = ag.at[it, s, down(k), 1 - x, c, :, cols]
+            arrived(block, agx_s.at[it, s, ch, k], agx_r.at[it, s, ch, k], across)
+        line = ag.at[it, s, :, 1 - x, c, :, cols]
+        send(line, line, agc_s.at[it, s, ch, 1], agc_r.at[it, s, ch, 1], sibling)
+
+    def halves(it, s, ch):
+        cols = pl.ds(ch * width, width)
+        arrived(ag.at[it, s, :, x, 1 - c, :, cols], agc_s.at[it, s, ch, 0], agc_r.at[it, s, ch, 0], sibling)
+        arrived(ag.at[it, s, :, 1 - x, 1 - c, :, cols], agc_s.at[it, s, ch, 1], agc_r.at[it, s, ch, 1], sibling)
+        if not ready[0]:
+            ready[0] = True
+            loads[3].wait()
+        gathered = ag[it, s, :, :, :, :, cols].reshape(nocc, width)
         product = jnp.dot(occ_v[...].reshape(local_aux * nocc, nocc), gathered, preferred_element_type=F32)
         for p in range(local_aux):
-            half[:, pl.ds(p * nvir, nvir)] = product[p * nocc : (p + 1) * nocc].astype(BF16)
-
-    def turn(p):
-        loads[4 + p].wait()
-        vir_t[pl.ds(p * nvir, nvir), :] = vir_v[p].T
+            half[s, :, pl.ds(p * nvir + ch * width, width)] = product[p * nocc : (p + 1) * nocc].astype(BF16)
 
     def exchange(it, s, ch):
         cols = pl.ds(ch * width, width)
-        product = jnp.dot(half[...], vir_t[:, cols], preferred_element_type=F32)
+        if not ready[1]:
+            ready[1] = True
+            for load in loads[4:]:
+                load.wait()
+        product = lax.dot_general(
+            half[s], vir_v[cols, :], (((1,), (1,)), ((), ())), preferred_element_type=F32
+        )
         ex[it, s, :, :, :, :, cols] = product.reshape(nz, 2, 2, rows, width)
         send(
             ex.at[it, s, :, :, 1 - c, :, cols], cr.at[it, s, :, :, :, cols],
@@ -147,63 +154,81 @@
             )
         zo[s, :, cols] = xo[s, z, :, cols] + xr[it, s, z, :, cols].astype(F32)
 
-    def rs_end(it, s):
-        for ch in range(CHUNKS):
-            cols = pl.ds(ch * width, width)
-            total = zo[s, :, cols]
-            for k in near_first:
-                arrived(zr.at[it, s, k, :, cols], rz_s.at[it, s, ch, k], rz_r.at[it, s, ch, k], dev(down(k), x, c))
-                total = total + zr[it, s, k, :, cols].astype(F32)
-            new = 0.4 * resp[s, :, cols] + 0.6 * (rhs[:, s, cols] - total) / denom[:, cols]
-            if it == ITERS - 1:
-                out[:, s, cols] = new
-            else:
-                resp[s, :, cols] = new
-
-    a, b = 0, 1
-    ag_start(0, a)
-    ag_start(0, b)
-    first, second = local_aux // 2, local_aux
-    for p in range(first):
-        turn(p)
-    ag_z(0, a)
-    for p in range(first, second):
-        turn(p)
-    ag_x(0, a)
-    ag_z(0, b)
-    ag_c(0, a)
-    loads[3].wait()
-    for it in range(ITERS):
-        halves(it, a)
-        if it > 0:
-            ag_z(it, b)
-        exchange(it, a, 0)
-        ag_x(it, b)
-        exchange(it, a, 1)
-        rs_x(it, a, 0)
-        ag_c(it, b)
-        halves(it, b)
-        rs_x(it, a, 1)
-        rs_z(it, a, 0)
-        exchange(it, b, 0)
-        rs_z(it, a, 1)
-        rs_x(it, b, 0)
-        exchange(it, b, 1)
-        rs_end(it, a)
-        if it + 1 < ITERS:
-            ag_start(it + 1, a)
-        rs_x(it, b, 1)
-        rs_z(it, b, 0)
-        rs_z(it, b, 1)
-        if it + 1 < ITERS:
-            ag_z(it + 1, a)
-        rs_end(it, b)
-        if it + 1 < ITERS:
-            ag_start(it + 1, b)
-            ag_x(it + 1, a)
-            ag_c(it + 1, a)
+    def update(it, s, ch):
+        cols = pl.ds(ch * width, width)
+        total = zo[s, :, cols]
+        for k in near_first:
+            arrived(zr.at[it, s, k, :, cols], rz_s.at[it, s, ch, k], rz_r.at[it, s, ch, k], dev(down(k), x, c))
+            total = total + zr[it, s, k, :, cols].astype(F32)
+        new = 0.4 * resp[s, :, cols] + 0.6 * (rhs[:, s, cols] - total) / denom[:, cols]
+        if it == ITERS - 1:
+            out[:, s, cols] = new
+        else:
+            resp[s, :, cols] = new
+            ag_start(it + 1, s, ch)
+
+    ready = [False, False]
+    steps = dict(
+        ag_start=ag_start, ag_z=ag_z, ag_x=ag_x, halves=halves,
+        exchange=exchange, rs_x=rs_x, rs_z=rs_z, update=update,
+    )
+    for name, it, s, ch in plan(states):
+        steps[name](it, s, ch)
     for copy in sent:
         copy.wait_send()
+
+
+def plan(states):
+    units = states * CHUNKS
+    link, core, hop, near = 10500 // units // 2, 1800 // units, 1000, 700
+    took = dict(
+        ag_start=150, ag_z=200, ag_x=100, halves=1100 // units,
+        exchange=4400 // units, rs_x=200, rs_z=200, update=250,
+    )
+    free, order, now = dict(x=0, z=0, c=0), [], 0
+
+    def carry(lane, begin, length, latency):
+        free[lane] = max(free[lane], begin) + length
+        return free[lane] + latency
+
+    todo = [("ag_start", 0, s, ch) for s in range(states) for ch in range(CHUNKS)]
+    for it in range(ITERS):
+        for name in ("ag_z", "ag_x", "halves", "exchange", "rs_x", "rs_z", "update"):
+            todo += [(name, it, s, ch) for s in range(states) for ch in range(CHUNKS)]
+    arrival = {}
+    done = set()
+    while todo:
+
+        def rank(step):
+            name, it, s, ch = step
+            if name == "exchange":
+                needs = [("halves", it, s, each) in done for each in range(CHUNKS)]
+                begin = 0 if all(needs) else 1 << 40
+            else:
+                begin = 0 if name == "ag_start" else arrival.get(step, 1 << 40)
+            return (max(now, begin), name in ("halves", "exchange"), s, it, ch)
+
+        step = min(todo, key=rank)
+        name, it, s, ch = step
+        now = max(now, rank(step)[0]) + took[name]
+        todo.remove(step)
+        done.add(step)
+        order.append(step)
+        if name == "ag_start" or (name == "update" and it + 1 < ITERS):
+            ahead = it + (name == "update")
+            arrival[("ag_z", ahead, s, ch)] = carry("z", now, link, hop)
+            carry("x", now, link // 4, hop)
+        elif name == "ag_z":
+            arrival[("ag_x", it, s, ch)] = carry("x", now, link * 3 // 4, hop)
+        elif name == "ag_x":
+            arrival[("halves", it, s, ch)] = carry("c", now, core // 4, near)
+        elif name == "exchange":
+            arrival[("rs_x", it, s, ch)] = carry("c", now, core, near)
+        elif name == "rs_x":
+            arrival[("rs_z", it, s, ch)] = carry("x", now, link, hop)
+        elif name == "rs_z":
+            arrival[("update", it, s, ch)] = carry("z", now, link, hop)
+    return order
 
 
 def fused(rhs, occ_energy, vir_energy, occ_ints, vir_ints, devices):
@@ -226,12 +251,11 @@
             pltpu.VMEM((1, nocc), F32),
             pltpu.VMEM((1, nvir), F32),
             pltpu.VMEM(occ_ints.shape, BF16),
-            pltpu.VMEM(vir_ints.shape, BF16),
-            pltpu.VMEM((local_aux * nvir, nvir), BF16),
+            pltpu.VMEM((nvir, local_aux * nvir), BF16),
             pltpu.VMEM((rows, nvir), F32),
             pltpu.VMEM((states, rows, nvir), F32),
             pltpu.VMEM(lead + (nz, 2, 2, rows, nvir), BF16),
-            pltpu.VMEM((nocc, local_aux * nvir), BF16),
+            pltpu.VMEM((states, nocc, local_aux * nvir), BF16),
             pltpu.VMEM(lead + (nz, 2, 2, rows, nvir), F32),
             pltpu.VMEM(lead + (nz, 2, rows, nvir), F32),
             pltpu.VMEM((states, nz, rows, nvir), F32),
@@ -241,11 +265,11 @@
             pltpu.VMEM(lead + (nz, rows, nvir), BF16),
             pltpu.VMEM(lead + (nz, rows, nvir), BF16),
             dma((local_aux + 4,)),
-            *pair(nz), *pair(nz), *pair(2),
+            *pair(CHUNKS, nz), *pair(CHUNKS, nz), *pair(CHUNKS, 2),
             *pair(CHUNKS), *pair(CHUNKS), *pair(CHUNKS, nz),
         ],
         compiler_params=pltpu.CompilerParams(
-            collective_id=0, has_side_effects=True, vmem_limit_bytes=52 * 2**20
+            collective_id=0, has_side_effects=True, vmem_limit_bytes=62 * 2**20
         ),
         cost_estimate=pl.CostEstimate(flops=flops, bytes_accessed=2 * vir_ints.size, transcendentals=0),
     )(rhs, occ_energy.reshape(1, nocc), vir_energy.reshape(1, nvir), occ_ints, vir_ints)

time: 67.3 us -> 61.3 us (0.911)
  Pallas kernels: 63.1 us -> 59.5 us
  local copies, waits for them, and re-layouts: 3.97 us -> 1.57 us
    pallas_call x1, Pallas kernels: 63.1 us -> 59.5 us  [fused(): pl.pallas_call(functools.partial(kernel, nz), out_shape=jax.ShapeDtypeStr...]
    unnamed x9 -> x1, local copies, waits for them, and re-layouts: 3.97 us -> 1.57 us
where the time goes in v1:
time: 61.3 us; the launch traced here: 61.1 us
  Pallas kernels  59.5 us (97%)
  local copies, waits for them, and re-layouts  1.57 us (3%)
    pallas_call x1, Pallas kernels, fused(): pl.pallas_call(functools.partial(kernel, nz), out_shape=jax.ShapeDtypeStr...  59.5 us
    unnamed x1, local copies, waits for them, and re-layouts  1.57 us

profile of v1, /device:TPU:0, one launch (start us, length us, event | category | flops | bytes accessed | tf_op | source)
XLA Modules:
  0.0 61.1 jit_solution(10139030192611851504)
XLA Ops:
  0.0 59.5 %shard_map.55 = f32[16,2,1024]{2,1,0:T(2,128)} custom-call(f32[16,2,1024]{2,1,0:T(2,128)} %rhs_hbm.1, f32[1,256]{1,0:T(1,128)} %bitcast.3, f32[1,1024]{1,0:T(1,128)} %bitcast.2, bf16[4,256,256]{2,1,0:T(8,128)(2,1)} %occ_hbm.1, bf16[4,1024,1024]{2,1,0:T(8,128)(2,1)} %vir_hbm.1), custom_call_target="tpu_custom_call" | custom-call | flops 10737418240 | bytes 8388608 | tf_op jit(solution)/shard_map/pallas_call | solution.py:244
  59.6 1.6 %copy.7 = f32[16,2,1024]{2,1,0:T(2,128)} copy(f32[16,2,1024]{2,1,0:T(2,128)} %shard_map.55) | data formatting | bytes 262144

commit v2 on v1

--- a/solution.py
+++ b/solution.py
@@ -8,7 +8,7 @@
 from jax.sharding import PartitionSpec as P
 
 ITERS = 2
-CHUNKS = 2
+CHUNKS = 1
 MESH = pl.DeviceIdType.MESH
 F32 = jnp.float32
 BF16 = jnp.bfloat16
@@ -16,7 +16,7 @@
 
 def kernel(
     nz, rhs_hbm, occ_e_hbm, vir_e_hbm, occ_hbm, vir_hbm, out,
-    rhs, occ_e, vir_e, occ_v, vir_v, denom, resp, ag, half, ex, cr, xo, xs, xr, zo, zs, zr,
+    rhs, occ_e, vir_e, occ_v, vir_v, denom, right, resp, ag, half, ex, cr, xo, xs, xr, zo, zs, zr,
     load_sem, agz_s, agz_r, agx_s, agx_r, agc_s, agc_r,
     rc_s, rc_r, rx_s, rx_r, rz_s, rz_r,
 ):
@@ -60,7 +60,8 @@
     own_occ = jnp.sum(jnp.where(picked, occ_e[...], 0.0), axis=1, keepdims=True)
     denom[...] = vir_e[...] - own_occ
     for s in range(states):
-        resp[s] = rhs[:, s, :] / denom[...]
+        right[s] = rhs[:, s, :]
+        resp[s] = right[s] / denom[...]
     pl.semaphore_wait(barrier, nz + 1)
 
     sent = []
@@ -160,7 +161,7 @@
         for k in near_first:
             arrived(zr.at[it, s, k, :, cols], rz_s.at[it, s, ch, k], rz_r.at[it, s, ch, k], dev(down(k), x, c))
             total = total + zr[it, s, k, :, cols].astype(F32)
-        new = 0.4 * resp[s, :, cols] + 0.6 * (rhs[:, s, cols] - total) / denom[:, cols]
+        new = 0.4 * resp[s, :, cols] + 0.6 * (right[s, :, cols] - total) / denom[:, cols]
         if it == ITERS - 1:
             out[:, s, cols] = new
         else:
@@ -254,6 +255,7 @@
             pltpu.VMEM((nvir, local_aux * nvir), BF16),
             pltpu.VMEM((rows, nvir), F32),
             pltpu.VMEM((states, rows, nvir), F32),
+            pltpu.VMEM((states, rows, nvir), F32),
             pltpu.VMEM(lead + (nz, 2, 2, rows, nvir), BF16),
             pltpu.VMEM((states, nocc, local_aux * nvir), BF16),
             pltpu.VMEM(lead + (nz, 2, 2, rows, nvir), F32),

time: 61.3 us -> 63.6 us (1.038)
  Pallas kernels: 59.5 us -> 61.9 us
    pallas_call x1, Pallas kernels: 59.5 us -> 61.9 us  [fused(): pl.pallas_call(functools.partial(kernel, nz), out_shape=jax.ShapeDtypeStr...]
where the time goes in v2:
time: 63.6 us; the launch traced here: 63.5 us
  Pallas kernels  61.9 us (97%)
  local copies, waits for them, and re-layouts  1.57 us (2%)
    pallas_call x1, Pallas kernels, fused(): pl.pallas_call(functools.partial(kernel, nz), out_shape=jax.ShapeDtypeStr...  61.9 us
    unnamed x1, local copies, waits for them, and re-layouts  1.57 us

profile of v2, /device:TPU:0, one launch (start us, length us, event | category | flops | bytes accessed | tf_op | source)
XLA Modules:
  0.0 63.5 jit_solution(1447629958825463963)
XLA Ops:
  0.0 61.9 %shard_map.55 = f32[16,2,1024]{2,1,0:T(2,128)} custom-call(f32[16,2,1024]{2,1,0:T(2,128)} %rhs_hbm.1, f32[1,256]{1,0:T(1,128)} %bitcast.3, f32[1,1024]{1,0:T(1,128)} %bitcast.2, bf16[4,256,256]{2,1,0:T(8,128)(2,1)} %occ_hbm.1, bf16[4,1024,1024]{2,1,0:T(8,128)(2,1)} %vir_hbm.1), custom_call_target="tpu_custom_call" | custom-call | flops 10737418240 | bytes 8388608 | tf_op jit(solution)/shard_map/pallas_call | solution.py:245
  61.9 1.6 %copy.7 = f32[16,2,1024]{2,1,0:T(2,128)} copy(f32[16,2,1024]{2,1,0:T(2,128)} %shard_map.55) | data formatting | bytes 262144

commit v3 on v2

--- a/solution.py
+++ b/solution.py
@@ -8,7 +8,7 @@
 from jax.sharding import PartitionSpec as P
 
 ITERS = 2
-CHUNKS = 1
+CHUNKS = 2
 MESH = pl.DeviceIdType.MESH
 F32 = jnp.float32
 BF16 = jnp.bfloat16
@@ -86,23 +86,20 @@
         block[...] = resp[s, :, cols].astype(BF16)
         for k in near_first[::-1]:
             send(block, block, agz_s.at[it, s, ch, k], agz_r.at[it, s, ch, k], dev(up(k), x, c))
-        send(block, block, agx_s.at[it, s, ch, 0], agx_r.at[it, s, ch, 0], across)
 
     def ag_z(it, s, ch):
         cols = pl.ds(ch * width, width)
         for k in near_first:
             block = ag.at[it, s, down(k), x, c, :, cols]
             arrived(block, agz_s.at[it, s, ch, k], agz_r.at[it, s, ch, k], dev(down(k), x, c))
-            send(block, block, agx_s.at[it, s, ch, k], agx_r.at[it, s, ch, k], across)
         line = ag.at[it, s, :, x, c, :, cols]
+        send(line, line, agx_s.at[it, s, ch], agx_r.at[it, s, ch], across)
         send(line, line, agc_s.at[it, s, ch, 0], agc_r.at[it, s, ch, 0], sibling)
 
     def ag_x(it, s, ch):
         cols = pl.ds(ch * width, width)
-        for k in [0] + near_first:
-            block = ag.at[it, s, down(k), 1 - x, c, :, cols]
-            arrived(block, agx_s.at[it, s, ch, k], agx_r.at[it, s, ch, k], across)
         line = ag.at[it, s, :, 1 - x, c, :, cols]
+        arrived(line, agx_s.at[it, s, ch], agx_r.at[it, s, ch], across)
         send(line, line, agc_s.at[it, s, ch, 1], agc_r.at[it, s, ch, 1], sibling)
 
     def halves(it, s, ch):
@@ -169,22 +166,30 @@
             ag_start(it + 1, s, ch)
 
     ready = [False, False]
+    retired = 0
     steps = dict(
         ag_start=ag_start, ag_z=ag_z, ag_x=ag_x, halves=halves,
         exchange=exchange, rs_x=rs_x, rs_z=rs_z, update=update,
     )
-    for name, it, s, ch in plan(states):
+    order = plan(states)
+    begun = []
+    for at, (name, it, s, ch) in enumerate(order):
+        begun.append(len(sent))
+        if at >= len(order) - 8:
+            while retired < begun[at - 8]:
+                sent[retired].wait_send()
+                retired += 1
         steps[name](it, s, ch)
-    for copy in sent:
+    for copy in sent[retired:]:
         copy.wait_send()
 
 
 def plan(states):
     units = states * CHUNKS
-    link, core, hop, near = 10500 // units // 2, 1800 // units, 1000, 700
+    link, core, hop, near = 10500 // units // 2, 1800 // units, 1500, 1000
     took = dict(
-        ag_start=150, ag_z=200, ag_x=100, halves=1100 // units,
-        exchange=4400 // units, rs_x=200, rs_z=200, update=250,
+        ag_start=500, ag_z=400, ag_x=200, halves=1600 // units,
+        exchange=7000 // units, rs_x=300, rs_z=500, update=700,
     )
     free, order, now = dict(x=0, z=0, c=0), [], 0
 
@@ -218,9 +223,8 @@
         if name == "ag_start" or (name == "update" and it + 1 < ITERS):
             ahead = it + (name == "update")
             arrival[("ag_z", ahead, s, ch)] = carry("z", now, link, hop)
-            carry("x", now, link // 4, hop)
         elif name == "ag_z":
-            arrival[("ag_x", it, s, ch)] = carry("x", now, link * 3 // 4, hop)
+            arrival[("ag_x", it, s, ch)] = carry("x", now, link, hop)
         elif name == "ag_x":
             arrival[("halves", it, s, ch)] = carry("c", now, core // 4, near)
         elif name == "exchange":
@@ -267,7 +271,7 @@
             pltpu.VMEM(lead + (nz, rows, nvir), BF16),
             pltpu.VMEM(lead + (nz, rows, nvir), BF16),
             dma((local_aux + 4,)),
-            *pair(CHUNKS, nz), *pair(CHUNKS, nz), *pair(CHUNKS, 2),
+            *pair(CHUNKS, nz), *pair(CHUNKS), *pair(CHUNKS, 2),
             *pair(CHUNKS), *pair(CHUNKS), *pair(CHUNKS, nz),
         ],
         compiler_params=pltpu.CompilerParams(

time: 63.6 us -> 59.6 us (0.937)
  Pallas kernels: 61.9 us -> 57.9 us
    pallas_call x1, Pallas kernels: 61.9 us -> 57.9 us  [fused(): pl.pallas_call(functools.partial(kernel, nz), out_shape=jax.ShapeDtypeStr...]
where the time goes in v3:
time: 59.6 us; the launch traced here: 59.5 us
  Pallas kernels  57.9 us (97%)
  local copies, waits for them, and re-layouts  1.57 us (3%)
    pallas_call x1, Pallas kernels, fused(): pl.pallas_call(functools.partial(kernel, nz), out_shape=jax.ShapeDtypeStr...  57.9 us
    unnamed x1, local copies, waits for them, and re-layouts  1.57 us

profile of v3, /device:TPU:0, one launch (start us, length us, event | category | flops | bytes accessed | tf_op | source)
XLA Modules:
  0.0 59.5 jit_solution(7023053676801406926)
XLA Ops:
  0.0 57.9 %shard_map.55 = f32[16,2,1024]{2,1,0:T(2,128)} custom-call(f32[16,2,1024]{2,1,0:T(2,128)} %rhs_hbm.1, f32[1,256]{1,0:T(1,128)} %bitcast.3, f32[1,1024]{1,0:T(1,128)} %bitcast.2, bf16[4,256,256]{2,1,0:T(8,128)(2,1)} %occ_hbm.1, bf16[4,1024,1024]{2,1,0:T(8,128)(2,1)} %vir_hbm.1), custom_call_target="tpu_custom_call" | custom-call | flops 10737418240 | bytes 8388608 | tf_op jit(solution)/shard_map/pallas_call | solution.py:249
  57.9 1.6 %copy.7 = f32[16,2,1024]{2,1,0:T(2,128)} copy(f32[16,2,1024]{2,1,0:T(2,128)} %shard_map.55) | data formatting | bytes 262144

commit v4 on v3

--- a/solution.py
+++ b/solution.py
@@ -114,20 +114,22 @@
         for p in range(local_aux):
             half[s, :, pl.ds(p * nvir + ch * width, width)] = product[p * nocc : (p + 1) * nocc].astype(BF16)
 
-    def exchange(it, s, ch):
+    def exchange(it, _, ch):
         cols = pl.ds(ch * width, width)
         if not ready[1]:
             ready[1] = True
             for load in loads[4:]:
                 load.wait()
         product = lax.dot_general(
-            half[s], vir_v[cols, :], (((1,), (1,)), ((), ())), preferred_element_type=F32
+            half[...].reshape(states * nocc, local_aux * nvir), vir_v[cols, :], (((1,), (1,)), ((), ())), preferred_element_type=F32
         )
-        ex[it, s, :, :, :, :, cols] = product.reshape(nz, 2, 2, rows, width)
-        send(
-            ex.at[it, s, :, :, 1 - c, :, cols], cr.at[it, s, :, :, :, cols],
-            rc_s.at[it, s, ch], rc_r.at[it, s, ch], sibling,
-        )
+        for s in range(states):
+            part = product[s * nocc : (s + 1) * nocc]
+            ex[it, s, :, :, :, :, cols] = part.reshape(nz, 2, 2, rows, width)
+            send(
+                ex.at[it, s, :, :, 1 - c, :, cols], cr.at[it, s, :, :, :, cols],
+                rc_s.at[it, s, ch], rc_r.at[it, s, ch], sibling,
+            )
 
     def rs_x(it, s, ch):
         cols = pl.ds(ch * width, width)
@@ -189,7 +191,7 @@
     link, core, hop, near = 10500 // units // 2, 1800 // units, 1500, 1000
     took = dict(
         ag_start=500, ag_z=400, ag_x=200, halves=1600 // units,
-        exchange=7000 // units, rs_x=300, rs_z=500, update=700,
+        exchange=5000 // CHUNKS, rs_x=300, rs_z=500, update=700,
     )
     free, order, now = dict(x=0, z=0, c=0), [], 0
 
@@ -200,7 +202,8 @@
     todo = [("ag_start", 0, s, ch) for s in range(states) for ch in range(CHUNKS)]
     for it in range(ITERS):
         for name in ("ag_z", "ag_x", "halves", "exchange", "rs_x", "rs_z", "update"):
-            todo += [(name, it, s, ch) for s in range(states) for ch in range(CHUNKS)]
+            own = range(1 if name == "exchange" else states)
+            todo += [(name, it, s, ch) for s in own for ch in range(CHUNKS)]
     arrival = {}
     done = set()
     while todo:
@@ -208,7 +211,7 @@
         def rank(step):
             name, it, s, ch = step
             if name == "exchange":
-                needs = [("halves", it, s, each) in done for each in range(CHUNKS)]
+                needs = [("halves", it, t, each) in done for t in range(states) for each in range(CHUNKS)]
                 begin = 0 if all(needs) else 1 << 40
             else:
                 begin = 0 if name == "ag_start" else arrival.get(step, 1 << 40)
@@ -228,7 +231,8 @@
         elif name == "ag_x":
             arrival[("halves", it, s, ch)] = carry("c", now, core // 4, near)
         elif name == "exchange":
-            arrival[("rs_x", it, s, ch)] = carry("c", now, core, near)
+            for t in range(states):
+                arrival[("rs_x", it, t, ch)] = carry("c", now, core, near)
         elif name == "rs_x":
             arrival[("rs_z", it, s, ch)] = carry("x", now, link, hop)
         elif name == "rs_z":

time: 59.6 us -> 66.3 us (1.11)
  Pallas kernels: 57.9 us -> 64.6 us
    pallas_call x1, Pallas kernels: 57.9 us -> 64.6 us  [fused(): pl.pallas_call(functools.partial(kernel, nz), out_shape=jax.ShapeDtypeStr...]
where the time goes in v4:
time: 66.3 us; the launch traced here: 66.2 us
  Pallas kernels  64.6 us (97%)
  local copies, waits for them, and re-layouts  1.57 us (2%)
    pallas_call x1, Pallas kernels, fused(): pl.pallas_call(functools.partial(kernel, nz), out_shape=jax.ShapeDtypeStr...  64.6 us
    unnamed x1, local copies, waits for them, and re-layouts  1.57 us

profile of v4, /device:TPU:0, one launch (start us, length us, event | category | flops | bytes accessed | tf_op | source)
XLA Modules:
  0.0 66.2 jit_solution(16116152290671113475)
XLA Ops:
  0.0 64.6 %shard_map.55 = f32[16,2,1024]{2,1,0:T(2,128)} custom-call(f32[16,2,1024]{2,1,0:T(2,128)} %rhs_hbm.1, f32[1,256]{1,0:T(1,128)} %bitcast.3, f32[1,1024]{1,0:T(1,128)} %bitcast.2, bf16[4,256,256]{2,1,0:T(8,128)(2,1)} %occ_hbm.1, bf16[4,1024,1024]{2,1,0:T(8,128)(2,1)} %vir_hbm.1), custom_call_target="tpu_custom_call" | custom-call | flops 10737418240 | bytes 8388608 | tf_op jit(solution)/shard_map/pallas_call | solution.py:253
  64.6 1.6 %copy.7 = f32[16,2,1024]{2,1,0:T(2,128)} copy(f32[16,2,1024]{2,1,0:T(2,128)} %shard_map.55) | data formatting | bytes 262144

commit v5 on v3

--- a/solution.py
+++ b/solution.py
@@ -211,7 +211,9 @@
                 needs = [("halves", it, s, each) in done for each in range(CHUNKS)]
                 begin = 0 if all(needs) else 1 << 40
             else:
-                begin = 0 if name == "ag_start" else arrival.get(step, 1 << 40)
+                begin = arrival.get(step, 1 << 40)
+                if name == "ag_start":
+                    begin = 0 if s == 0 or ("ag_z", 0, s - 1, 0) in done else 1 << 40
             return (max(now, begin), name in ("halves", "exchange"), s, it, ch)
 
         step = min(todo, key=rank)

time: 59.6 us -> 59.1 us (level)
  no operation moved by 1% of the time
where the time goes in v5:
time: 59.1 us; the launch traced here: 59 us
  Pallas kernels  57.4 us (97%)
  local copies, waits for them, and re-layouts  1.57 us (3%)
    pallas_call x1, Pallas kernels, fused(): pl.pallas_call(functools.partial(kernel, nz), out_shape=jax.ShapeDtypeStr...  57.4 us
    unnamed x1, local copies, waits for them, and re-layouts  1.57 us

profile of v5, /device:TPU:0, one launch (start us, length us, event | category | flops | bytes accessed | tf_op | source)
XLA Modules:
  0.0 59.0 jit_solution(17850516065540212151)
XLA Ops:
  0.0 57.4 %shard_map.55 = f32[16,2,1024]{2,1,0:T(2,128)} custom-call(f32[16,2,1024]{2,1,0:T(2,128)} %rhs_hbm.1, f32[1,256]{1,0:T(1,128)} %bitcast.3, f32[1,1024]{1,0:T(1,128)} %bitcast.2, bf16[4,256,256]{2,1,0:T(8,128)(2,1)} %occ_hbm.1, bf16[4,1024,1024]{2,1,0:T(8,128)(2,1)} %vir_hbm.1), custom_call_target="tpu_custom_call" | custom-call | flops 10737418240 | bytes 8388608 | tf_op jit(solution)/shard_map/pallas_call | solution.py:251
  57.4 1.6 %copy.7 = f32[16,2,1024]{2,1,0:T(2,128)} copy(f32[16,2,1024]{2,1,0:T(2,128)} %shard_map.55) | data formatting | bytes 262144
